TPU v7x, 512 devices: a whole 4x8x8 slice. The times are simulated.
512 devices in a mesh: dp: 4 (over y_lo, core), expert: 128 (over x, y_hi, z).
Axes of the slice: x: 4, y: 8 (y_hi: 4, y_lo: 2; y = y_hi * 2 + y_lo), z: 8, core: 2. Of those that a mesh axis runs over, the one named last changes fastest.
Arguments:
- tokens: bfloat16 [512, 256, 640], P(('dp', 'expert')), may hold values from -96 to 96
- slot_keys: bfloat16 [640, 128], replicated, may hold values from -1 to 1
- w_input: bfloat16 [128, 640, 2560], P('expert', None, 'dp'), may hold values from -0.25 to 0.25
- w_output: bfloat16 [128, 2560, 640], P('expert', 'dp'), may hold values from -0.125 to 0.125
- output_grad: bfloat16 [512, 256, 640], P(('dp', 'expert')), may hold values from -6 to 6
Outputs:
- grad_tokens: bfloat16 [512, 256, 640], P(('dp', 'expert'))
- grad_slot_keys: float32 [640, 128], replicated
- grad_w_input: bfloat16 [128, 640, 2560], P('expert', None, 'dp')
- grad_w_output: bfloat16 [128, 2560, 640], P('expert', 'dp')
All inputs are finite; a program needn't handle non-finite values.
Results may differ from a plain program's by a relative error of at most 0.025.
Values may be sent and summed in bfloat16 or wider, within the bound.
A program may use at most 64 MiB of HBM per device.

v0:
```python
import jax
import jax.numpy as jnp
from jax import lax
from jax.sharding import PartitionSpec as P


def gelu_back(pre_act, upstream):
    value, pullback = jax.vjp(jax.nn.gelu, pre_act)
    return pullback(upstream)[0]


def expert_local(rows_in, rows_grad, w_input, w_output):
    pre_act = jnp.einsum("red,edh->reh", rows_in, w_input, preferred_element_type=jnp.float32)
    activated = jax.nn.gelu(pre_act).astype(jnp.bfloat16)
    act_grad = jnp.einsum("red,ehd->reh", rows_grad, w_output, preferred_element_type=jnp.float32)
    pre_grad = gelu_back(pre_act, act_grad).astype(jnp.bfloat16)
    grad_w_output = jnp.einsum(
        "reh,red->ehd", activated, rows_grad, preferred_element_type=jnp.float32
    ).astype(jnp.bfloat16)
    grad_w_input = jnp.einsum(
        "red,reh->edh", rows_in, pre_grad, preferred_element_type=jnp.float32
    ).astype(jnp.bfloat16)
    return (activated, pre_grad, grad_w_input, grad_w_output)


def partial_pair(activated, pre_grad, w_input, w_output):
    out_part = jnp.einsum("reh,ehd->red", activated, w_output, preferred_element_type=jnp.float32)
    in_part = jnp.einsum("reh,edh->red", pre_grad, w_input, preferred_element_type=jnp.float32)
    return (out_part, in_part)


def body(tokens, slot_keys, w_input, w_output, output_grad):
    logits = jnp.einsum("bmd,ds->bms", tokens, slot_keys, preferred_element_type=jnp.float32)
    dispatch = jax.nn.softmax(logits, axis=1)
    combine = jax.nn.softmax(logits, axis=2)
    dispatch_low = dispatch.astype(jnp.bfloat16)
    combine_low = combine.astype(jnp.bfloat16)
    slot_in = jnp.einsum(
        "bms,bmd->bsd", dispatch_low, tokens, preferred_element_type=jnp.float32
    ).astype(jnp.bfloat16)
    slot_grad = jnp.einsum(
        "bms,bmd->bsd", combine_low, output_grad, preferred_element_type=jnp.float32
    ).astype(jnp.bfloat16)
    group_in, group_grad = (
        lax.all_gather(slot_in, "dp", axis=0, tiled=True),
        lax.all_gather(slot_grad, "dp", axis=0, tiled=True),
    )
    rows_in, rows_grad = (
        lax.all_to_all(group_in, "expert", split_axis=1, concat_axis=0, tiled=True),
        lax.all_to_all(group_grad, "expert", split_axis=1, concat_axis=0, tiled=True),
    )
    activated, pre_grad, grad_w_input, grad_w_output = expert_local(
        rows_in, rows_grad, w_input, w_output
    )
    out_part, in_part = partial_pair(activated, pre_grad, w_input, w_output)
    out_back, in_back = (
        lax.all_to_all(
            out_part.astype(jnp.bfloat16), "expert", split_axis=0, concat_axis=1, tiled=True
        ),
        lax.all_to_all(
            in_part.astype(jnp.bfloat16), "expert", split_axis=0, concat_axis=1, tiled=True
        ),
    )
    out_total, in_total = (
        lax.psum_scatter(
            out_back.astype(jnp.float32).astype(jnp.bfloat16), "dp", scatter_dimension=0, tiled=True
        ).astype(jnp.float32),
        lax.psum_scatter(
            in_back.astype(jnp.float32).astype(jnp.bfloat16), "dp", scatter_dimension=0, tiled=True
        ).astype(jnp.float32),
    )
    slot_out = out_total.astype(jnp.bfloat16)
    slot_in_grad = in_total.astype(jnp.bfloat16)
    combine_grad = jnp.einsum(
        "bmd,bsd->bms", output_grad, slot_out, preferred_element_type=jnp.float32
    )
    dispatch_grad = jnp.einsum(
        "bmd,bsd->bms", tokens, slot_in_grad, preferred_element_type=jnp.float32
    )
    logit_grad = combine * (combine_grad - jnp.sum(combine * combine_grad, axis=2, keepdims=True))
    logit_grad = logit_grad + dispatch * (
        dispatch_grad - jnp.sum(dispatch * dispatch_grad, axis=1, keepdims=True)
    )
    logit_grad = logit_grad.astype(jnp.bfloat16)
    grad_tokens = jnp.einsum(
        "bms,bsd->bmd", dispatch_low, slot_in_grad, preferred_element_type=jnp.float32
    )
    grad_tokens = grad_tokens + jnp.einsum(
        "bms,ds->bmd", logit_grad, slot_keys, preferred_element_type=jnp.float32
    )
    key_term = jnp.einsum("bmd,bms->ds", tokens, logit_grad, preferred_element_type=jnp.float32)
    grad_slot_keys = lax.psum(key_term, ("dp", "expert"))
    return (grad_tokens.astype(jnp.bfloat16), grad_slot_keys, grad_w_input, grad_w_output)


def solution(mesh):
    placed = (
        P(("dp", "expert"), None, None),
        P(),
        P("expert", None, "dp"),
        P("expert", "dp", None),
        P(("dp", "expert"), None, None),
    )
    return jax.shard_map(
        body,
        mesh=mesh,
        in_specs=placed,
        out_specs=(
            P(("dp", "expert"), None, None),
            P(),
            P("expert", None, "dp"),
            P("expert", "dp", None),
        ),
        check_vma=False,
    )
```

profile of v0, /device:TPU:1, one launch (start us, length us, event | category | flops | bytes accessed | tf_op | source)
XLA Modules:
  0.0 488.1 jit_solution(14730509305306180026)
XLA Ops:
  7.2 0.0 copy-start
  7.2 1.4 fusion.41
  8.6 0.0 copy-start.2
  8.6 0.2 fusion.34
  8.8 1.2 convolution_convert_fusion.4
  10.0 13.6 %all-gather.1 = bf16[512,640]{1,0:T(8,128)(2,1)S(1)} all-gather(bf16[128,640]{1,0:T(8,128)(2,1)S(1)} %convolution_convert_fusion.4), channel_id=3, replica_groups=mesh['dp'=4,'expert'=128] {'dp'}, dimensions={0}, use_global_device_ids=true | all-gather | bytes 819200 | tf_op jit(solution)/shard_map/all_gather | solution.py:45
  23.6 1.3 copy.34
  25.0 15.2 %all-to-all-start.1 = ((bf16[4,128,640]{2,0,1:T(4,128)(2,1)}), bf16[4,128,640]{2,0,1:T(4,128)(2,1)S(1)}, u32[]{:S(2)}, u32[]{:S(2)}) async-start(bf16[4,128,640]{2,0,1:T(4,128)(2,1)} %copy.34), calls=%async_computation.1 | async-start | bytes 1310720 | tf_op jit(solution)/shard_map/all_to_all | solution.py:49
  40.2 0.4 convolution_convert_fusion.5
  40.6 19.4 %all-gather = bf16[512,640]{1,0:T(8,128)(2,1)S(1)} all-gather(bf16[128,640]{1,0:T(8,128)(2,1)S(1)} %convolution_convert_fusion.5), channel_id=2, replica_groups=mesh['dp'=4,'expert'=128] {'dp'}, dimensions={0}, use_global_device_ids=true | all-gather | bytes 819200 | tf_op jit(solution)/shard_map/all_gather | solution.py:46
  60.0 1.3 copy.33
  61.3 1.9 all-to-all-done.1
  63.2 13.6 %all-to-all-start = ((bf16[4,128,640]{2,0,1:T(4,128)(2,1)}), bf16[4,128,640]{2,0,1:T(4,128)(2,1)S(1)}, u32[]{:S(2)}, u32[]{:S(2)}) async-start(bf16[4,128,640]{2,0,1:T(4,128)(2,1)} %copy.33), calls=%async_computation | async-start | bytes 1310720 | tf_op jit(solution)/shard_map/all_to_all | solution.py:50
  76.8 0.0 reduce-scatter.3.cloned.1.call-start
  76.8 0.1 reshape.134
  77.0 23.0 %all-to-all-done = bf16[4,128,640]{2,0,1:T(4,128)(2,1)S(1)} async-done(((bf16[4,128,640]{2,0,1:T(4,128)(2,1)}), bf16[4,128,640]{2,0,1:T(4,128)(2,1)S(1)}, u32[]{:S(2)}, u32[]{:S(2)}) %all-to-all-start) | async-done | bytes 655392 | tf_op jit(solution)/shard_map/all_to_all | solution.py:50
  100.0 0.1 reshape.132
  100.2 0.0 copy-start.11
  100.2 0.7 convolution_bitcast_fusion
  101.0 0.1 copy-done.7
  101.1 0.5 copy-done.11
  101.6 1.2 fusion.13
  102.8 0.8 copy-done.14
  103.7 0.8 fusion.9
  104.5 0.5 broadcast.69
  105.0 1.1 reduce.14
  106.1 0.4 reshape.144
  106.5 33.2 %all_to_all.66 = bf16[128,2,1280]{2,1,0:T(2,128)(2,1)S(1)} all-to-all(bf16[128,2,1280]{2,1,0:T(2,128)(2,1)S(1)} %reshape.144), channel_id=1, replica_groups=mesh['dp'=4,'expert'=128] {'expert'}, dimensions={0} | all-to-all | bytes 1310720 | tf_op jit(solution)/shard_map/all_to_all | solution.py:60
  139.7 0.5 reshape.145
  140.2 4.0 reduce.12
  144.2 0.2 all_to_all.55
  144.4 0.9 copy.36
  145.3 0.0 reduce-scatter.3.cloned.1.call-update
  145.3 0.0 reduce-scatter.5.cloned.1.call-start
  145.4 0.6 copy-done.5
  145.9 2.9 fusion.10
  148.8 2.2 reduce.15
  151.0 0.4 reshape.146
  151.4 31.7 %all_to_all.67 = bf16[128,2,1280]{2,1,0:T(2,128)(2,1)S(1)} all-to-all(bf16[128,2,1280]{2,1,0:T(2,128)(2,1)S(1)} %reshape.146), channel_id=1, replica_groups=mesh['dp'=4,'expert'=128] {'expert'}, dimensions={0} | all-to-all | bytes 1310720 | tf_op jit(solution)/shard_map/all_to_all | solution.py:57
  183.2 0.5 reshape.147
  183.7 4.0 reduce.13
  187.7 0.2 all_to_all.59
  187.8 0.9 copy.38
  188.8 0.0 reduce-scatter.5.cloned.1.call-update
  188.8 0.0 copy-start.6
  188.8 0.0 all-reduce.2.cloned.1.call-start
  188.9 2.8 fusion.7
  191.7 0.0 copy-done.8
  191.7 0.0 copy-start.13
  191.7 1.7 fusion.8
  193.4 0.0 copy-done.1
  193.4 1.2 convolution_bitcast_fusion.3
  194.6 10.6 %reduce-scatter.5.cloned.1.call-done = bf16[1,128,640]{2,1,0:T(8,128)(2,1)} async-done(((bf16[4,128,640]{2,1,0:T(8,128)(2,1)}), bf16[1,128,640]{2,1,0:T(8,128)(2,1)}) %reduce-scatter.5.cloned.1.call-update) | async-done | bytes 163856 | tf_op jit(solution)/shard_map/reduce_scatter | solution.py:65
  205.2 0.0 copy-done.13
  205.2 1.3 multiply_reduce_fusion.1
  206.4 0.0 copy-start.9
  206.5 0.2 add_convert_fusion
  206.6 1.0 convolution_bitcast_fusion.2
  207.6 0.0 all-reduce.2.cloned.1.call-update
  207.6 0.2 fusion.29
  207.9 0.0 copy-done.9
  207.9 1.0 fusion.12
  208.8 270.9 %all-reduce.2.cloned.1.call-done = f32[640,128]{0,1:T(8,128)} async-done(((f32[640,128]{0,1:T(8,128)}), f32[640,128]{0,1:T(8,128)}) %all-reduce.2.cloned.1.call-update) | async-done | bytes 327696 | tf_op jit(solution)/shard_map/psum | solution.py:92
  479.7 1.9 copy.41
  (17 shorter events, 0.0 us)
Async XLA Ops:
  7.2 93.0 %copy-start = (bf16[1,640,640]{2,1,0:T(8,128)(2,1)S(1)}, bf16[1,640,640]{2,1,0:T(8,128)(2,1)}, u32[]{:S(2)}) copy-start(bf16[1,640,640]{2,1,0:T(8,128)(2,1)} %param.7) | copy-start | bytes 2457604
  8.6 31.6 %copy-start.2 = (f32[256,128]{1,0:T(8,128)}, f32[256,128]{1,0:T(8,128)S(1)}, u32[]{:S(2)}) copy-start(f32[256,128]{1,0:T(8,128)S(1)} %get-tuple-element.30) | copy-start | bytes 393220
  23.6 16.6 %copy-start.12 = (bf16[1,256,640]{2,1,0:T(8,128)(2,1)S(1)}, bf16[1,256,640]{2,1,0:T(8,128)(2,1)}, u32[]{:S(2)}) copy-start(bf16[1,256,640]{2,1,0:T(8,128)(2,1)} %param.9) | copy-start | bytes 983044
  25.0 38.2 %all-to-all-start.1 = ((bf16[4,128,640]{2,0,1:T(4,128)(2,1)}), bf16[4,128,640]{2,0,1:T(4,128)(2,1)S(1)}, u32[]{:S(2)}, u32[]{:S(2)}) async-start(bf16[4,128,640]{2,0,1:T(4,128)(2,1)} %copy.34), calls=%async_computation.1 | async-start | bytes 1310720 | tf_op jit(solution)/shard_map/all_to_all | solution.py:49
  63.2 36.8 %all-to-all-start = ((bf16[4,128,640]{2,0,1:T(4,128)(2,1)}), bf16[4,128,640]{2,0,1:T(4,128)(2,1)S(1)}, u32[]{:S(2)}, u32[]{:S(2)}) async-start(bf16[4,128,640]{2,0,1:T(4,128)(2,1)} %copy.33), calls=%async_computation | async-start | bytes 1310720 | tf_op jit(solution)/shard_map/all_to_all | solution.py:50
  76.8 116.6 %reduce-scatter.3.cloned.1.call-start = ((), (), s32[]{:S(2)}) async-start(), calls=%async_computation.6 | async-start | bytes 819200 | tf_op jit(solution)/shard_map/reduce_scatter | solution.py:68
  100.2 0.9 copy-start.7
  100.2 1.4 copy-start.11
  101.6 1.2 copy-start.4
  102.8 0.8 copy-start.14
  144.4 1.6 copy-start.5
  145.3 59.8 %reduce-scatter.5.cloned.1.call-start = ((), (), s32[]{:S(2)}) async-start(), calls=%async_computation.7 | async-start | bytes 819200 | tf_op jit(solution)/shard_map/reduce_scatter | solution.py:65
  188.8 2.9 copy-start.6
  188.8 290.9 %all-reduce.2.cloned.1.call-start = ((), (), s32[]{:S(2)}) async-start(), calls=%async_computation.8 | async-start | bytes 655360 | tf_op jit(solution)/shard_map/psum | solution.py:92
  188.8 2.8 copy-start.8
  191.7 1.7 copy-start.1
  191.7 13.5 %copy-start.3 = (f32[256,128]{1,0:T(8,128)S(1)}, f32[256,128]{1,0:T(8,128)}, u32[]{:S(2)}) copy-start(f32[256,128]{1,0:T(8,128)} %copy-done.2) | copy-start | bytes 393220
  191.7 13.5 %copy-start.13 = (bf16[1,256,640]{2,1,0:T(8,128)(2,1)S(1)}, bf16[1,256,640]{2,1,0:T(8,128)(2,1)}, u32[]{:S(2)}) copy-start(bf16[1,256,640]{2,1,0:T(8,128)(2,1)} %param.9) | copy-start | bytes 983044
  194.6 13.0 %copy-start.10 = (bf16[1,128,640]{2,1,0:T(8,128)(2,1)S(1)}, bf16[1,128,640]{2,1,0:T(8,128)(2,1)}, u32[]{:S(2)}) copy-start(bf16[1,128,640]{2,1,0:T(8,128)(2,1)} %reduce-scatter.3.cloned.1.call-done) | copy-start | bytes 491524
  206.4 1.4 copy-start.9
Sparse Core Ops, SparseCore 0:
  145.5 22.7 reduce-scatter.2
  188.9 16.2 reduce-scatter.4
  210.7 268.9 all-reduce.1
where the time goes:
time: 490 us; the launch traced here: 488 us
  waiting for transfers between devices  306 us (62%)
  blocking collectives  97.9 us (20%)
  starting transfers between devices  28.9 us (6%)
  matrix products  17.7 us (4%)
  between operations  14.1 us (3%)
  other arithmetic  11.6 us (2%)
  local copies, waits for them, and re-layouts  11.5 us (2%)
    psum x1, waiting for transfers between devices, body(): grad_slot_keys = lax.psum(key_term, ('dp', 'expert'))  271 us
    all_to_all x1, blocking collectives, body(): lax.all_to_all(in_part.astype(jnp.bfloat16), 'expert', split_axis=0, conc...  33.2 us
    all_to_all x1, blocking collectives, body(): lax.all_to_all(out_part.astype(jnp.bfloat16), 'expert', split_axis=0, con...  31.7 us
    all_to_all x1, waiting for transfers between devices, body(): lax.all_to_all(group_grad, 'expert', split_axis=1, concat_axis=0, tiled=T...  23 us
    all_gather x1, blocking collectives, body(): lax.all_gather(slot_grad, 'dp', axis=0, tiled=True)  19.4 us
    all_to_all x1, starting transfers between devices, body(): lax.all_to_all(group_in, 'expert', split_axis=1, concat_axis=0, tiled=True)  15.2 us
    all_gather x1, blocking collectives, body(): lax.all_gather(slot_in, 'dp', axis=0, tiled=True)  13.6 us
    all_to_all x1, starting transfers between devices, body(): lax.all_to_all(group_grad, 'expert', split_axis=1, concat_axis=0, tiled=T...  13.6 us
  transfers between devices with their start and end apart: 5, of which 4 were waited for; matrix products, arithmetic and copies ran while one was open for 4% of the time, Pallas kernels for 0%

commit v1 on v0

v1 whole, which is shorter than its diff:
```python
import functools

import jax
import jax.numpy as jnp
from jax import lax
from jax.experimental import pallas as pl
from jax.experimental.pallas import tpu as pltpu
from jax.sharding import PartitionSpec as P

MESH = pl.DeviceIdType.MESH
F32 = jnp.float32
BF16 = jnp.bfloat16
NX, NY, NZ = 4, 4, 8
NE = NX * NY * NZ
D = 640
TALL = (((0,), (0,)), ((), ()))
WIDE = (((1,), (1,)), ((), ()))


def dot(a, b, dims=(((1,), (0,)), ((), ()))):
    return lax.dot_general(a, b, dims, preferred_element_type=F32)


def gelu_pair(v):
    c = 0.7978845608028654
    sq = v * v
    t = jnp.tanh(c * (v + 0.044715 * (sq * v)))
    half = 0.5 * (1.0 + t)
    slope = half + 0.5 * v * (1.0 - t * t) * (c * (1.0 + 3.0 * 0.044715 * sq))
    return v * half, slope


def interleaver():
    r = lax.broadcasted_iota(jnp.int32, (256, 256), 0)
    c = lax.broadcasted_iota(jnp.int32, (256, 256), 1)
    return (r == 2 * (c - 128 * (c >= 128).astype(jnp.int32)) + (c >= 128).astype(jnp.int32)).astype(BF16)


def kernel(
    tok_ref, keys_ref, wi_hbm, wo_hbm, og_ref,
    gt_ref, gk_ref, gwi_ref, gwo_ref,
    wi, wo, dispatch, combine, mix,
    src1, dst1, rows, act, pre_grad, part, sib_in, chip_sum, par_in, src2, dst2,
    key_mine, key_sib, key_split, key_got, key_row, key_rows, key_all,
    w_sem, a1_s, a1_r, g_s, g_r, p_s, p_r, c_s, c_r, a2_s, a2_r,
    k_s, k_r,
):
    g = lax.axis_index("dp")
    e = lax.axis_index("expert")
    core, ylo = g % 2, g // 2
    x, y, z = e // (NY * NZ), (e // NZ) % NY, e % NZ
    sib = (g + 1 - 2 * core, e)
    par = ((g + 2) % 4, e)
    diag = ((g + 3 - 2 * core) % 4, e)

    def nth(k):
        dz = (k % 2) * 4 + ((k // 8) % 2) * 2 + (k // 64) % 2
        dy = ((k // 2) % 2) * 2 + (k // 16) % 2
        dx = ((k // 4) % 2) * 2 + (k // 32) % 2
        return ((x + dx) % NX) * (NY * NZ) + ((y + dy) % NY) * NZ + (z + dz) % NZ

    def plane(k):
        dx, dz = k // NZ, k % NZ
        return ((x + dx) % NX), (z + dz) % NZ

    def line(k):
        yy = (2 * y + ylo + k) % 8
        return ((yy % 2) * 2 + core, x * (NY * NZ) + (yy // 2) * NZ + z)

    def copy(src, dst, s, r, dev):
        return pltpu.make_async_remote_copy(
            src_ref=src, dst_ref=dst, send_sem=s, recv_sem=r,
            device_id=dev, device_id_type=MESH,
        )

    load_i = pltpu.make_async_copy(wi_hbm, wi, w_sem.at[0])
    load_o = pltpu.make_async_copy(wo_hbm, wo, w_sem.at[1])
    load_i.start()
    load_o.start()

    barrier = pltpu.get_barrier_semaphore()

    def greet(k, _):
        pl.semaphore_signal(barrier, inc=1, device_id=(g, (e + k) % NE), device_id_type=MESH)
        return 0

    lax.fori_loop(1, NE, greet, 0)
    for dev in (sib, par, diag):
        pl.semaphore_signal(barrier, inc=1, device_id=dev, device_id_type=MESH)
    for k in range(1, NY):
        other = ((g + 2) % 4, x * (NY * NZ) + ((y + k) % NY) * NZ + z)
        pl.semaphore_signal(barrier, inc=1, device_id=other, device_id_type=MESH)

    tok = tok_ref[...]
    logits = dot(tok, keys_ref[...])
    ex = jnp.exp(logits - jnp.max(logits, axis=0, keepdims=True))
    disp = ex / jnp.sum(ex, axis=0, keepdims=True)
    ex = jnp.exp(logits - jnp.max(logits, axis=1, keepdims=True))
    comb = ex / jnp.sum(ex, axis=1, keepdims=True)
    dispatch[...] = disp
    combine[...] = comb
    slot_in = dot(disp.astype(BF16), tok, TALL).astype(BF16)
    slot_grad = dot(comb.astype(BF16), og_ref[...], TALL).astype(BF16)
    mix[...] = interleaver()
    pair = dot(mix[...], jnp.concatenate([slot_in, slot_grad], axis=0)).astype(BF16)
    src1[...] = pair.reshape(NE, 2, D)
    dst1[pl.ds(e, 1)] = src1[pl.ds(e, 1)]

    pl.semaphore_wait(barrier, NE - 1 + 3 + NY - 1)

    def exchange(src, dst, s, r):
        def step(k, _):
            t = nth(k)
            copy(src.at[t], dst.at[e], s, r, (g, t)).start()
            return 0

        lax.fori_loop(1, NE, step, 0)
        return copy(src.at[pl.ds(0, NE - 1)], dst.at[pl.ds(0, NE - 1)], s, r, sib)

    done1 = exchange(src1, dst1, a1_s, a1_r)
    done1.wait_recv()

    both = dot(mix[...], dst1[...].reshape(2 * NE, D), TALL).astype(BF16)
    rows[0, 0] = both[:NE]
    rows[1, 0] = both[NE:]
    to_par = copy(rows.at[:, 0], rows.at[:, 2], g_s.at[1], g_r.at[1], par)
    to_par.start()
    to_sib = copy(rows.at[:, 0], rows.at[:, 1], g_s.at[0], g_r.at[0], sib)
    to_sib.start()
    fwd = copy(rows.at[:, 2], rows.at[:, 3], g_s.at[2], g_r.at[2], sib)

    load_i.wait()
    load_o.wait()

    def expert(r):
        value, slope = gelu_pair(dot(rows[0, r], wi[...]))
        value = value.astype(BF16)
        act[r] = value
        down = (dot(rows[1, r], wo[...], WIDE) * slope).astype(BF16)
        pre_grad[r] = down
        part[0, r] = dot(value, wo[...]).astype(BF16)
        part[1, r] = dot(down, wi[...], WIDE).astype(BF16)

    expert(0)
    to_sib.wait_recv()
    expert(1)
    give1 = copy(part.at[:, 1], sib_in.at[:, 0], p_s.at[0], p_r.at[0], sib)
    give1.start()
    to_par.wait_recv()
    fwd.start()
    expert(2)
    fwd.wait_recv()
    expert(3)
    give3 = copy(part.at[:, 3], sib_in.at[:, 1], p_s.at[1], p_r.at[1], sib)
    give3.start()
    give3.wait_recv()
    chip_sum[...] = (part[:, 2].astype(F32) + sib_in[:, 1].astype(F32)).astype(BF16)
    cross = copy(chip_sum, par_in, c_s, c_r, par)
    cross.start()

    gwo_ref[...] = dot(act[...].reshape(4 * NE, D), rows[1].reshape(4 * NE, D), TALL).astype(BF16)
    gwi_ref[...] = dot(rows[0].reshape(4 * NE, D), pre_grad[...].reshape(4 * NE, D), TALL).astype(BF16)

    give1.wait_recv()
    near = part[:, 0].astype(F32) + sib_in[:, 0].astype(F32)
    cross.wait_recv()
    total = (near + par_in[...].astype(F32)).astype(BF16).reshape(2 * NE, D)
    src2[...] = dot(mix[...], total).astype(BF16).reshape(NE, 2, D)
    dst2[pl.ds(e, 1)] = src2[pl.ds(e, 1)]
    done2 = exchange(src2, dst2, a2_s, a2_r)
    done2.wait_recv()

    both = dot(mix[...], dst2[...].reshape(2 * NE, D), TALL).astype(BF16)
    slot_out, slot_in_grad = both[:NE], both[NE:]
    tok = tok_ref[...]
    cg = dot(og_ref[...], slot_out, WIDE)
    dg = dot(tok, slot_in_grad, WIDE)
    comb = combine[...]
    disp = dispatch[...]
    lg = comb * (cg - jnp.sum(comb * cg, axis=1, keepdims=True))
    lg = lg + disp * (dg - jnp.sum(disp * dg, axis=0, keepdims=True))
    lg = lg.astype(BF16)
    term = dot(lg, tok, TALL)

    half = NE // 2
    key_mine[...] = term.reshape(2, half, D)
    k0 = copy(key_mine.at[1 - core], key_sib, k_s.at[0], k_r.at[0], sib)
    k0.start()
    grad = dot(disp.astype(BF16), slot_in_grad) + dot(lg, keys_ref[...], WIDE)
    gt_ref[...] = grad.astype(BF16)
    k0.wait_recv()
    mine = x * NZ + z
    nxz = NX * NZ
    key_split[...] = (key_mine[core] + key_sib[...]).reshape(nxz, 2, D)

    def plane_copy(src, dst, i, k):
        xx, zz = plane(k)
        return copy(src(xx * NZ + zz), dst, k_s.at[i], k_r.at[i], (g, xx * (NY * NZ) + y * NZ + zz))

    def scatter(k, _):
        plane_copy(lambda t: key_split.at[t], key_got.at[mine], 1, k).start()
        return 0

    lax.fori_loop(1, nxz, scatter, 0)
    key_got[pl.ds(mine, 1)] = key_split[pl.ds(mine, 1)]
    k1 = copy(key_split.at[pl.ds(0, nxz - 1)], key_got.at[pl.ds(0, nxz - 1)], k_s.at[1], k_r.at[1], sib)
    k1.wait_recv()
    row = jnp.sum(key_got[...], axis=0)
    place = 2 * y + ylo
    key_row[...] = row
    key_rows[pl.ds(place, 1)] = row[None]

    for k in range(1, 8):
        copy(key_row, key_rows.at[place], k_s.at[2], k_r.at[2], line(k)).start()
    k2 = copy(key_rows.at[pl.ds(0, 7)], key_rows.at[pl.ds(0, 7)], k_s.at[2], k_r.at[2], sib)
    k2.wait_recv()
    row = jnp.sum(key_rows[...], axis=0)
    k2.wait_send()
    key_row[...] = row
    key_all[pl.ds(core * nxz + mine, 1)] = row[None]

    def spread(k, _):
        plane_copy(lambda t: key_row, key_all.at[core * nxz + mine], 3, k).start()
        return 0

    lax.fori_loop(1, nxz, spread, 0)
    k3 = copy(key_split.at[pl.ds(0, nxz - 1)], key_got.at[pl.ds(0, nxz - 1)], k_s.at[3], k_r.at[3], sib)
    k3.wait_recv()
    own = key_all.at[pl.ds(core * nxz, nxz)]
    k4 = copy(own, own, k_s.at[4], k_r.at[4], sib)
    k4.start()
    k4.wait_recv()
    gk_ref[...] = key_all[...].reshape(NE, D)

    done1.wait_send()
    to_par.wait_send()
    to_sib.wait_send()
    fwd.wait_send()
    give1.wait_send()
    give3.wait_send()
    cross.wait_send()
    done2.wait_send()
    k0.wait_send()
    k1.wait_send()
    k3.wait_send()
    k4.wait_send()


def body(tokens, slot_keys, w_input, w_output, output_grad):
    vm = pl.BlockSpec(memory_space=pltpu.VMEM)
    anywhere = pl.BlockSpec(memory_space=pl.ANY)
    dma = pltpu.SemaphoreType.DMA
    n = NE
    gt, gk, gwi, gwo = pl.pallas_call(
        kernel,
        out_shape=(
            jax.ShapeDtypeStruct((256, D), BF16),
            jax.ShapeDtypeStruct((n, D), F32),
            jax.ShapeDtypeStruct((D, D), BF16),
            jax.ShapeDtypeStruct((D, D), BF16),
        ),
        in_specs=[vm, vm, anywhere, anywhere, vm],
        out_specs=[vm] * 4,
        scratch_shapes=[
            pltpu.VMEM((D, D), BF16),
            pltpu.VMEM((D, D), BF16),
            pltpu.VMEM((256, n), F32),
            pltpu.VMEM((256, n), F32),
            pltpu.VMEM((256, 256), BF16),
            pltpu.VMEM((n, 2, D), BF16),
            pltpu.VMEM((n, 2, D), BF16),
            pltpu.VMEM((2, 4, n, D), BF16),
            pltpu.VMEM((4, n, D), BF16),
            pltpu.VMEM((4, n, D), BF16),
            pltpu.VMEM((2, 4, n, D), BF16),
            pltpu.VMEM((2, 2, n, D), BF16),
            pltpu.VMEM((2, n, D), BF16),
            pltpu.VMEM((2, n, D), BF16),
            pltpu.VMEM((n, 2, D), BF16),
            pltpu.VMEM((n, 2, D), BF16),
            pltpu.VMEM((2, n // 2, D), F32),
            pltpu.VMEM((n // 2, D), F32),
            pltpu.VMEM((NX * NZ, 2, D), F32),
            pltpu.VMEM((NX * NZ, 2, D), F32),
            pltpu.VMEM((2, D), F32),
            pltpu.VMEM((8, 2, D), F32),
            pltpu.VMEM((2 * NX * NZ, 2, D), F32),
            dma((2,)), dma, dma, dma((3,)), dma((3,)), dma((2,)), dma((2,)), dma, dma, dma, dma,
            dma((5,)), dma((5,)),
        ],
        compiler_params=pltpu.CompilerParams(
            collective_id=0, has_side_effects=True, vmem_limit_bytes=40 << 20
        ),
    )(tokens[0], slot_keys, w_input[0], w_output[0], output_grad[0])
    return gt[None], gk.T, gwi[None], gwo[None]


def solution(mesh):
    placed = (
        P(("dp", "expert"), None, None),
        P(),
        P("expert", None, "dp"),
        P("expert", "dp", None),
        P(("dp", "expert"), None, None),
    )
    return jax.shard_map(
        body,
        mesh=mesh,
        in_specs=placed,
        out_specs=(
            P(("dp", "expert"), None, None),
            P(),
            P("expert", None, "dp"),
            P("expert", "dp", None),
        ),
        check_vma=False,
    )
```

time: 490 us -> 100 us (0.20)
  waiting for transfers between devices: 306 us -> 0 us
  blocking collectives: 97.9 us -> 0 us
  Pallas kernels: 0 us -> 90.9 us
  starting transfers between devices: 28.9 us -> 0 us
  matrix products: 17.7 us -> 0 us
  between operations: 14.1 us -> 0.65 us
  other arithmetic: 11.6 us -> 0 us
    psum x1 -> x0, waiting for transfers between devices: 271 us -> none  [body(): grad_slot_keys = lax.psum(key_term, ('dp', 'expert'))]
    pallas_call x0 -> x1, Pallas kernels: none -> 90.9 us  [body(): pl.pallas_call(kernel, out_shape=(jax.ShapeDtypeStruct((256, D), BF16), j...]
    all_to_all x2 -> x0, blocking collectives: 64.9 us -> none  [the longest x1 33.2 us: body(): lax.all_to_all(in_part.astype(jnp.bfloat16), 'expert', split_axis=0, conc...]
    all_gather x2 -> x0, blocking collectives: 33 us -> none  [the longest x1 19.4 us: body(): lax.all_gather(slot_grad, 'dp', axis=0, tiled=True)]
    all_to_all x2 -> x0, starting transfers between devices: 28.8 us -> none  [the longest x1 15.2 us: body(): lax.all_to_all(group_in, 'expert', split_axis=1, concat_axis=0, tiled=True)]
    all_to_all x2 -> x0, waiting for transfers between devices: 24.9 us -> none  [the longest x1 23 us: body(): lax.all_to_all(group_grad, 'expert', split_axis=1, concat_axis=0, tiled=T...]
    dot_general x14 -> x0, matrix products: 17.7 us -> none  [the longest x1 2.86 us: partial_pair(): jnp.einsum('reh,ehd->red', activated, w_output, preferred_element_type=jn...]
    reduce_scatter x2 -> x0, waiting for transfers between devices: 10.6 us -> none  [the longest x1 10.6 us: body(): lax.psum_scatter(out_back.astype(jnp.float32).astype(jnp.bfloat16), 'dp',...]
  transfers between devices with their start and end apart: 5 -> 0, of which waited for: 4 -> 0; matrix products, arithmetic and copies ran while one was open for 4% -> 0% of each run, Pallas kernels for 0% -> 0%
where the time goes in v1:
time: 100 us
  Pallas kernels  90.9 us (91%)
  local copies, waits for them, and re-layouts  8.54 us (9%)
    pallas_call x1, Pallas kernels, body(): pl.pallas_call(kernel, out_shape=(jax.ShapeDtypeStruct((256, D), BF16), j...  90.9 us
    unnamed x14, local copies, waits for them, and re-layouts  8.54 us

profile of v1, /device:TPU:1, one launch (start us, length us, event | category | flops | bytes accessed | tf_op | source)
XLA Modules:
  0.0 100.1 jit_solution(513809766786001577)
XLA Ops:
  0.6 0.0 copy-start
  0.6 1.1 %copy-done = bf16[1,640,640]{2,1,0:T(8,128)(2,1)S(1)} copy-done((bf16[1,640,640]{2,1,0:T(8,128)(2,1)S(1)}, bf16[1,640,640]{2,1,0:T(8,128)(2,1)}, u32[]{:S(2)}) %copy-start) | copy-done | bytes 819224
  1.8 0.0 copy-start.1
  1.8 1.1 %copy-done.1 = bf16[1,640,640]{2,1,0:T(8,128)(2,1)S(1)} copy-done((bf16[1,640,640]{2,1,0:T(8,128)(2,1)S(1)}, bf16[1,640,640]{2,1,0:T(8,128)(2,1)}, u32[]{:S(2)}) %copy-start.1) | copy-done | bytes 819224
  2.9 0.0 copy-start.2
  2.9 1.0 copy-done.2
  3.9 0.0 copy-start.3
  3.9 1.0 copy-done.3
  4.9 0.0 copy-start.4
  4.9 0.9 copy-done.4
  5.8 90.9 %shard_map.84 = (bf16[256,640]{1,0:T(8,128)(2,1)S(1)}, f32[128,640]{1,0:T(8,128)S(1)}, bf16[640,640]{1,0:T(8,128)(2,1)S(1)}, bf16[640,640]{1,0:T(8,128)(2,1)S(1)}) custom-call(bf16[256,640]{1,0:T(8,128)(2,1)S(1)} %bitcast.12, bf16[640,128]{1,0:T(8,128)(2,1)S(1)} %copy-done.4, bf16[640,640]{1,0:T(8,128)(2,1)S(1)} %bitcast.8, bf16[640,640]{1,0:T(8,128)(2,1)S(1)} %bitcast.9, ...), custom_call_target="tpu_custom_call" | custom-call | tf_op jit(solution)/shard_map/pallas_call | solution.py:254
  96.7 0.9 copy.9
  97.6 0.7 copy.13
  98.3 0.9 copy.14
  99.2 0.9 copy.15
Async XLA Ops:
  0.6 1.1 %copy-start = (bf16[1,640,640]{2,1,0:T(8,128)(2,1)S(1)}, bf16[1,640,640]{2,1,0:T(8,128)(2,1)}, u32[]{:S(2)}) copy-start(bf16[1,640,640]{2,1,0:T(8,128)(2,1)} %param.7) | copy-start | bytes 2457604
  1.8 1.1 %copy-start.1 = (bf16[1,640,640]{2,1,0:T(8,128)(2,1)S(1)}, bf16[1,640,640]{2,1,0:T(8,128)(2,1)}, u32[]{:S(2)}) copy-start(bf16[1,640,640]{2,1,0:T(8,128)(2,1)} %param.8) | copy-start | bytes 2457604
  2.9 1.0 copy-start.2
  3.9 1.0 copy-start.3
  4.9 0.9 copy-start.4

commit v2 on v1

v2 whole, which is shorter than its diff:
```python
import functools

import jax
import jax.numpy as jnp
from jax import lax
from jax.experimental import pallas as pl
from jax.experimental.pallas import tpu as pltpu
from jax.sharding import PartitionSpec as P

MESH = pl.DeviceIdType.MESH
F32 = jnp.float32
BF16 = jnp.bfloat16
NX, NY, NZ = 4, 4, 8
NE = NX * NY * NZ
HALF = NE // 2
D = 640
TALL = (((0,), (0,)), ((), ()))
WIDE = (((1,), (1,)), ((), ()))


def dot(a, b, dims=(((1,), (0,)), ((), ()))):
    return lax.dot_general(a, b, dims, preferred_element_type=F32)


def gelu_pair(v):
    c = 0.7978845608028654
    sq = v * v
    t = jnp.tanh(c * (v + 0.044715 * (sq * v)))
    half = 0.5 * (1.0 + t)
    slope = half + 0.5 * v * (1.0 - t * t) * (c * (1.0 + 3.0 * 0.044715 * sq))
    return v * half, slope


def interleaver():
    r = lax.broadcasted_iota(jnp.int32, (2 * HALF, 2 * HALF), 0)
    c = lax.broadcasted_iota(jnp.int32, (2 * HALF, 2 * HALF), 1)
    p = (c >= HALF).astype(jnp.int32)
    return (r == 2 * (c - HALF * p) + p).astype(BF16)


def kernel(
    tok_hbm, keys_hbm, wi_hbm, wo_hbm, og_hbm,
    gt_hbm, gk_ref, gwi_hbm, gwo_hbm,
    tok_ref, keys_ref, wi, wo, og_ref, gt, gwi, gwo,
    dispatch, combine, mix,
    src1, dst1, rows, act, pre_grad, part, sib_in, chip_sum, par_in, src2, dst2,
    key_mine, key_sib, key_split, key_got, key_row, key_rows, key_low, key_all,
    w_sem, o_sem, a1_s, a1_r, g_s, g_r, p_s, p_r, c_s, c_r, a2_s, a2_r,
    k_s, k_r,
):
    g = lax.axis_index("dp")
    e = lax.axis_index("expert")
    core, ylo = g % 2, g // 2
    x, y, z = e // (NY * NZ), (e // NZ) % NY, e % NZ
    sib = (g + 1 - 2 * core, e)
    par = ((g + 2) % 4, e)
    diag = ((g + 3 - 2 * core) % 4, e)

    def nth(q, k):
        dy = ((k // 2) % 2) * 2 + (k // 16) % 2
        dx = ((k // 4) % 2) * 2 + (k // 32) % 2
        dz = 2 * ((k % 2) * 2 + (k // 8) % 2) + (q + dx + dy) % 2
        return ((x + dx) % NX) * (NY * NZ) + ((y + dy) % NY) * NZ + (z + dz) % NZ

    def plane(k):
        dx, dz = k // NZ, k % NZ
        return ((x + dx) % NX), (z + dz) % NZ

    def line(k):
        yy = (2 * y + ylo + k) % 8
        return ((yy % 2) * 2 + core, x * (NY * NZ) + (yy // 2) * NZ + z)

    def copy(src, dst, s, r, dev):
        return pltpu.make_async_remote_copy(
            src_ref=src, dst_ref=dst, send_sem=s, recv_sem=r,
            device_id=dev, device_id_type=MESH,
        )

    loads = [
        pltpu.make_async_copy(far, near, w_sem.at[i])
        for i, (far, near) in enumerate((
            (tok_hbm, tok_ref), (keys_hbm, keys_ref), (og_hbm, og_ref), (wi_hbm, wi), (wo_hbm, wo)
        ))
    ]
    for load in loads:
        load.start()

    barrier = pltpu.get_barrier_semaphore()

    def greet(k, _):
        pl.semaphore_signal(barrier, inc=1, device_id=(g, (e + k) % NE), device_id_type=MESH)
        return 0

    lax.fori_loop(1, NE, greet, 0)
    for dev in (sib, par, diag):
        pl.semaphore_signal(barrier, inc=1, device_id=dev, device_id_type=MESH)
    for k in range(1, NY):
        other = ((g + 2) % 4, x * (NY * NZ) + ((y + k) % NY) * NZ + z)
        pl.semaphore_signal(barrier, inc=1, device_id=other, device_id_type=MESH)

    mix[...] = interleaver()

    def pairs(top, low):
        return dot(mix[...], jnp.concatenate([top, low], axis=0)).astype(BF16).reshape(HALF, 2, D)

    def apart(both):
        two = dot(mix[...], both.reshape(2 * HALF, D), TALL).astype(BF16)
        return two[:HALF], two[HALF:]

    loads[0].wait()
    loads[1].wait()
    tok = tok_ref[...]
    logits = dot(tok, keys_ref[...])
    ex = jnp.exp(logits - jnp.max(logits, axis=0, keepdims=True))
    disp = ex / jnp.sum(ex, axis=0, keepdims=True)
    ex = jnp.exp(logits - jnp.max(logits, axis=1, keepdims=True))
    comb = ex / jnp.sum(ex, axis=1, keepdims=True)
    dispatch[...] = disp
    combine[...] = comb
    slot_in = dot(disp.astype(BF16), tok, TALL).astype(BF16)
    loads[2].wait()
    slot_grad = dot(comb.astype(BF16), og_ref[...], TALL).astype(BF16)
    src1[0:HALF] = pairs(slot_in[:HALF], slot_grad[:HALF])
    src1[HALF:NE] = pairs(slot_in[HALF:], slot_grad[HALF:])
    own = e // 2
    dst1[0, pl.ds(own, 1)] = src1[pl.ds(e, 1)]

    pl.semaphore_wait(barrier, NE - 1 + 3 + NY - 1)

    def out_half(q):
        def step(k, _):
            t = nth(q, k)
            copy(src1.at[t], dst1.at[q, own], a1_s.at[q], a1_r.at[q], (g, t)).start()
            return 0

        lax.fori_loop(1 - q, HALF, step, 0)
        some = pl.ds(0, HALF - 1 + q)
        return copy(src1.at[some], dst1.at[q, some], a1_s.at[q], a1_r.at[q], sib)

    def back_half(q):
        def step(k, _):
            t = nth(q, k)
            copy(src2.at[q, t // 2], dst2.at[e], a2_s, a2_r, (g, t)).start()
            return 0

        lax.fori_loop(1 - q, HALF, step, 0)

    outs = [out_half(q) for q in range(2)]
    to_par = [copy(rows.at[:, q], rows.at[:, 4 + 2 * q], g_s.at[q], g_r.at[q], par) for q in range(2)]
    fwd = [
        copy(rows.at[:, 4 + 2 * q], rows.at[:, 5 + 2 * q], g_s.at[2 + q], g_r.at[2 + q], sib)
        for q in range(2)
    ]
    to_sib = copy(rows.at[:, pl.ds(0, 2)], rows.at[:, pl.ds(2, 2)], g_s.at[4], g_r.at[4], sib)
    for q in range(2):
        outs[q].wait_recv()
        rows[0, q], rows[1, q] = apart(dst1[q])
        to_par[q].start()
    to_sib.start()
    loads[3].wait()
    loads[4].wait()

    def expert(i):
        at = pl.ds(2 * i, 2)
        value, slope = gelu_pair(dot(rows[0, at].reshape(NE, D), wi[...]))
        value = value.astype(BF16)
        act[i] = value
        down = (dot(rows[1, at].reshape(NE, D), wo[...], WIDE) * slope).astype(BF16)
        pre_grad[i] = down
        part[0, at] = dot(value, wo[...]).astype(BF16).reshape(2, HALF, D)
        part[1, at] = dot(down, wi[...], WIDE).astype(BF16).reshape(2, HALF, D)

    give = [
        copy(part.at[:, 5 + 2 * q], sib_in.at[:, 2 + q], p_s.at[q], p_r.at[q], sib) for q in range(2)
    ]
    give_near = copy(part.at[:, pl.ds(2, 2)], sib_in.at[:, pl.ds(0, 2)], p_s.at[2], p_r.at[2], sib)
    cross = [copy(chip_sum.at[:, q], par_in.at[:, q], c_s.at[q], c_r.at[q], par) for q in range(2)]

    def add_up(q):
        give[q].wait_recv()
        chip_sum[:, q] = (part[:, 4 + 2 * q].astype(F32) + sib_in[:, 2 + q].astype(F32)).astype(BF16)
        cross[q].start()

    expert(0)
    to_par[0].wait_recv()
    fwd[0].start()
    to_sib.wait_recv()
    expert(1)
    give_near.start()
    fwd[0].wait_recv()
    expert(2)
    give[0].start()
    to_par[1].wait_recv()
    fwd[1].start()
    add_up(0)
    fwd[1].wait_recv()
    expert(3)
    give[1].start()
    add_up(1)

    store_o = pltpu.make_async_copy(gwo, gwo_hbm, o_sem.at[0])
    store_i = pltpu.make_async_copy(gwi, gwi_hbm, o_sem.at[1])
    store_t = pltpu.make_async_copy(gt, gt_hbm, o_sem.at[2])
    give_near.wait_recv()
    for q in range(2):
        near = part[:, q].astype(F32) + sib_in[:, q].astype(F32)
        cross[q].wait_recv()
        total = (near + par_in[:, q].astype(F32)).astype(BF16)
        src2[q] = pairs(total[0], total[1])
        if q == 0:
            dst2[pl.ds(e, 1)] = src2[0, pl.ds(own, 1)]
        back_half(q)
    backs = copy(dst2.at[pl.ds(0, NE - 1)], dst2.at[pl.ds(0, NE - 1)], a2_s, a2_r, sib)

    gwo[...] = dot(act[...].reshape(4 * NE, D), rows[1].reshape(4 * NE, D), TALL).astype(BF16)
    store_o.start()
    gwi[...] = dot(rows[0].reshape(4 * NE, D), pre_grad[...].reshape(4 * NE, D), TALL).astype(BF16)
    store_i.start()
    backs.wait_recv()

    low, high = apart(dst2[0:HALF]), apart(dst2[HALF:NE])
    slot_out = jnp.concatenate([low[0], high[0]], axis=0)
    slot_in_grad = jnp.concatenate([low[1], high[1]], axis=0)
    tok = tok_ref[...]
    cg = dot(og_ref[...], slot_out, WIDE)
    dg = dot(tok, slot_in_grad, WIDE)
    comb = combine[...]
    disp = dispatch[...]
    lg = comb * (cg - jnp.sum(comb * cg, axis=1, keepdims=True))
    lg = lg + disp * (dg - jnp.sum(disp * dg, axis=0, keepdims=True))
    lg = lg.astype(BF16)
    term = dot(lg, tok, TALL)

    key_mine[...] = term.reshape(2, HALF, D)
    k0 = copy(key_mine.at[1 - core], key_sib, k_s.at[0], k_r.at[0], sib)
    k0.start()
    grad = dot(disp.astype(BF16), slot_in_grad) + dot(lg, keys_ref[...], WIDE)
    gt[...] = grad.astype(BF16)
    store_t.start()
    k0.wait_recv()
    mine = x * NZ + z
    nxz = NX * NZ
    key_split[...] = (key_mine[core] + key_sib[...]).astype(BF16).reshape(nxz, 2, D)

    def plane_copy(src, dst, i, k):
        xx, zz = plane(k)
        return copy(src(xx * NZ + zz), dst, k_s.at[i], k_r.at[i], (g, xx * (NY * NZ) + y * NZ + zz))

    def scatter(k, _):
        plane_copy(lambda t: key_split.at[t], key_got.at[mine], 1, k).start()
        return 0

    lax.fori_loop(1, nxz, scatter, 0)
    key_got[pl.ds(mine, 1)] = key_split[pl.ds(mine, 1)]
    k1 = copy(key_split.at[pl.ds(0, nxz - 1)], key_got.at[pl.ds(0, nxz - 1)], k_s.at[1], k_r.at[1], sib)
    k1.wait_recv()
    row = jnp.sum(key_got[...].astype(F32), axis=0)
    place = 2 * y + ylo
    key_row[...] = row
    key_rows[pl.ds(place, 1)] = row[None]

    for k in range(1, 8):
        copy(key_row, key_rows.at[place], k_s.at[2], k_r.at[2], line(k)).start()
    k2 = copy(key_rows.at[pl.ds(0, 7)], key_rows.at[pl.ds(0, 7)], k_s.at[2], k_r.at[2], sib)
    k2.wait_recv()
    row = jnp.sum(key_rows[...], axis=0).astype(BF16)
    key_low[...] = row[None]
    key_all[pl.ds(core * nxz + mine, 1)] = row[None]

    def spread(k, _):
        plane_copy(lambda t: key_low.at[0], key_all.at[core * nxz + mine], 3, k).start()
        return 0

    lax.fori_loop(1, nxz, spread, 0)
    k3 = copy(key_split.at[pl.ds(0, nxz - 1)], key_got.at[pl.ds(0, nxz - 1)], k_s.at[3], k_r.at[3], sib)
    k3.wait_recv()
    held = key_all.at[pl.ds(core * nxz, nxz)]
    k4 = copy(held, held, k_s.at[4], k_r.at[4], sib)
    k4.start()
    k4.wait_recv()
    gk_ref[...] = key_all[...].reshape(NE, D)

    for store in (store_o, store_i, store_t):
        store.wait()
    for done in outs + to_par + fwd + [to_sib] + give + [give_near] + cross + [backs, k0, k1, k2, k3, k4]:
        done.wait_send()


def hand_over(gt, gk, gwi, gwo, gt_out, gk_out, gwi_out, gwo_out, sem):
    moves = [
        pltpu.make_async_copy(a, b, sem.at[i])
        for i, (a, b) in enumerate(((gwi, gwi_out), (gwo, gwo_out), (gt, gt_out)))
    ]
    for move in moves:
        move.start()
    gk_out[...] = gk[...].astype(F32).T
    for move in moves:
        move.wait()


def body(tokens, slot_keys, w_input, w_output, output_grad):
    vm = pl.BlockSpec(memory_space=pltpu.VMEM)
    anywhere = pl.BlockSpec(memory_space=pl.ANY)
    dma = pltpu.SemaphoreType.DMA
    n = NE
    gt, gk, gwi, gwo = pl.pallas_call(
        kernel,
        out_shape=(
            jax.ShapeDtypeStruct((256, D), BF16),
            jax.ShapeDtypeStruct((n, D), BF16),
            jax.ShapeDtypeStruct((D, D), BF16),
            jax.ShapeDtypeStruct((D, D), BF16),
        ),
        in_specs=[anywhere] * 5,
        out_specs=[anywhere, vm, anywhere, anywhere],
        scratch_shapes=[
            pltpu.VMEM((256, D), BF16),
            pltpu.VMEM((D, n), BF16),
            pltpu.VMEM((D, D), BF16),
            pltpu.VMEM((D, D), BF16),
            pltpu.VMEM((256, D), BF16),
            pltpu.VMEM((256, D), BF16),
            pltpu.VMEM((D, D), BF16),
            pltpu.VMEM((D, D), BF16),
            pltpu.VMEM((256, n), F32),
            pltpu.VMEM((256, n), F32),
            pltpu.VMEM((n, n), BF16),
            pltpu.VMEM((n, 2, D), BF16),
            pltpu.VMEM((2, HALF, 2, D), BF16),
            pltpu.VMEM((2, 8, HALF, D), BF16),
            pltpu.VMEM((4, n, D), BF16),
            pltpu.VMEM((4, n, D), BF16),
            pltpu.VMEM((2, 8, HALF, D), BF16),
            pltpu.VMEM((2, 4, HALF, D), BF16),
            pltpu.VMEM((2, 2, HALF, D), BF16),
            pltpu.VMEM((2, 2, HALF, D), BF16),
            pltpu.VMEM((2, HALF, 2, D), BF16),
            pltpu.VMEM((n, 2, D), BF16),
            pltpu.VMEM((2, HALF, D), F32),
            pltpu.VMEM((HALF, D), F32),
            pltpu.VMEM((NX * NZ, 2, D), BF16),
            pltpu.VMEM((NX * NZ, 2, D), BF16),
            pltpu.VMEM((2, D), F32),
            pltpu.VMEM((8, 2, D), F32),
            pltpu.VMEM((1, 2, D), BF16),
            pltpu.VMEM((2 * NX * NZ, 2, D), BF16),
            dma((5,)), dma((3,)), dma((2,)), dma((2,)), dma((5,)), dma((5,)), dma((3,)), dma((3,)),
            dma((2,)), dma((2,)), dma, dma,
            dma((5,)), dma((5,)),
        ],
        compiler_params=pltpu.CompilerParams(
            collective_id=0, has_side_effects=True, vmem_limit_bytes=60 << 20
        ),
    )(tokens[0], slot_keys, w_input[0], w_output[0], output_grad[0])
    gt, gk, gwi, gwo = pl.pallas_call(
        hand_over,
        out_shape=(
            jax.ShapeDtypeStruct((256, D), BF16),
            jax.ShapeDtypeStruct((D, n), F32),
            jax.ShapeDtypeStruct((D, D), BF16),
            jax.ShapeDtypeStruct((D, D), BF16),
        ),
        in_specs=[anywhere, vm, anywhere, anywhere],
        out_specs=[anywhere, vm, anywhere, anywhere],
        scratch_shapes=[dma((3,))],
    )(gt, gk, gwi, gwo)
    return gt[None], gk, gwi[None], gwo[None]


def solution(mesh):
    placed = (
        P(("dp", "expert"), None, None),
        P(),
        P("expert", None, "dp"),
        P("expert", "dp", None),
        P(("dp", "expert"), None, None),
    )
    return jax.shard_map(
        body,
        mesh=mesh,
        in_specs=placed,
        out_specs=(
            P(("dp", "expert"), None, None),
            P(),
            P("expert", None, "dp"),
            P("expert", "dp", None),
        ),
        check_vma=False,
    )
```

time: 100 us -> 144 us (1.44)
  Pallas kernels: 90.9 us -> 143 us
  local copies, waits for them, and re-layouts: 8.54 us -> 0 us
    pallas_call x0 -> x1, Pallas kernels: none -> 62.3 us  [body(): pl.pallas_call(hand_over, out_shape=(jax.ShapeDtypeStruct((256, D), BF16)...]
    pallas_call x1, Pallas kernels: 90.9 us -> 81 us  [body(): pl.pallas_call(kernel, out_shape=(jax.ShapeDtypeStruct((256, D), BF16), j...]
    unnamed x14 -> x0, local copies, waits for them, and re-layouts: 8.54 us -> none
where the time goes in v2:
time: 144 us
  Pallas kernels  143 us (99%)
    pallas_call x1, Pallas kernels, body(): pl.pallas_call(kernel, out_shape=(jax.ShapeDtypeStruct((256, D), BF16), j...  81 us
    pallas_call x1, Pallas kernels, body(): pl.pallas_call(hand_over, out_shape=(jax.ShapeDtypeStruct((256, D), BF16)...  62.3 us

profile of v2, /device:TPU:1, one launch (start us, length us, event | category | flops | bytes accessed | tf_op | source)
XLA Modules:
  0.0 143.9 jit_solution(11929496695823896580)
XLA Ops:
  0.6 81.0 %shard_map.84 = (bf16[256,640]{1,0:T(8,128)(2,1)}, bf16[128,640]{1,0:T(8,128)(2,1)}, bf16[640,640]{1,0:T(8,128)(2,1)}, bf16[640,640]{1,0:T(8,128)(2,1)}) custom-call(bf16[256,640]{1,0:T(8,128)(2,1)} %bitcast.9, bf16[640,128]{1,0:T(8,128)(2,1)} %keys_hbm.1, bf16[640,640]{1,0:T(8,128)(2,1)} %bitcast.7, bf16[640,640]{1,0:T(8,128)(2,1)} %bitcast.8, ...), custom_call_target="tpu_custom_call" | custom-call | tf_op jit(solution)/shard_map/pallas_call | solution.py:306
  81.6 62.3 %shard_map.85 = (bf16[256,640]{1,0:T(8,128)(2,1)}, f32[640,128]{1,0:T(8,128)}, bf16[640,640]{1,0:T(8,128)(2,1)}, bf16[640,640]{1,0:T(8,128)(2,1)}) custom-call(bf16[256,640]{1,0:T(8,128)(2,1)} %get-tuple-element.12.gt, bf16[128,640]{1,0:T(8,128)(2,1)} %get-tuple-element.13.gk, bf16[640,640]{1,0:T(8,128)(2,1)} %get-tuple-element.14.gwi, ...), custom_call_target="tpu_custom_call" | custom-call | tf_op jit(solution)/shard_map/pallas_call | solution.py:355

commit v3 on v2

--- a/solution.py
+++ b/solution.py
@@ -41,7 +41,7 @@
 def kernel(
     tok_hbm, keys_hbm, wi_hbm, wo_hbm, og_hbm,
     gt_hbm, gk_ref, gwi_hbm, gwo_hbm,
-    tok_ref, keys_ref, wi, wo, og_ref, gt, gwi, gwo,
+    tok_ref, keys_ref, wi, wo, og_ref, gt, gwi, gwo, wi_t, wo_t,
     dispatch, combine, mix,
     src1, dst1, rows, act, pre_grad, part, sib_in, chip_sum, par_in, src2, dst2,
     key_mine, key_sib, key_split, key_got, key_row, key_rows, key_low, key_all,
@@ -54,7 +54,6 @@
     x, y, z = e // (NY * NZ), (e // NZ) % NY, e % NZ
     sib = (g + 1 - 2 * core, e)
     par = ((g + 2) % 4, e)
-    diag = ((g + 3 - 2 * core) % 4, e)
 
     def nth(q, k):
         dy = ((k // 2) % 2) * 2 + (k // 16) % 2
@@ -62,13 +61,12 @@
         dz = 2 * ((k % 2) * 2 + (k // 8) % 2) + (q + dx + dy) % 2
         return ((x + dx) % NX) * (NY * NZ) + ((y + dy) % NY) * NZ + (z + dz) % NZ
 
-    def plane(k):
-        dx, dz = k // NZ, k % NZ
-        return ((x + dx) % NX), (z + dz) % NZ
-
-    def line(k):
-        yy = (2 * y + ylo + k) % 8
-        return ((yy % 2) * 2 + core, x * (NY * NZ) + (yy // 2) * NZ + z)
+    def near_by(k):
+        low, zz = (ylo + k // NZ) % 2, (z + k) % NZ
+        return low * NZ + zz, (low * 2 + core, x * (NY * NZ) + y * NZ + zz)
+
+    def far_off(k):
+        return (g, ((x + k // NY) % NX) * (NY * NZ) + ((y + k) % NY) * NZ + z)
 
     def copy(src, dst, s, r, dev):
         return pltpu.make_async_remote_copy(
@@ -92,11 +90,9 @@
         return 0
 
     lax.fori_loop(1, NE, greet, 0)
-    for dev in (sib, par, diag):
-        pl.semaphore_signal(barrier, inc=1, device_id=dev, device_id_type=MESH)
-    for k in range(1, NY):
-        other = ((g + 2) % 4, x * (NY * NZ) + ((y + k) % NY) * NZ + z)
-        pl.semaphore_signal(barrier, inc=1, device_id=other, device_id_type=MESH)
+    pl.semaphore_signal(barrier, inc=1, device_id=sib, device_id_type=MESH)
+    for k in range(NZ, 2 * NZ):
+        pl.semaphore_signal(barrier, inc=1, device_id=near_by(k)[1], device_id_type=MESH)
 
     mix[...] = interleaver()
 
@@ -125,7 +121,11 @@
     own = e // 2
     dst1[0, pl.ds(own, 1)] = src1[pl.ds(e, 1)]
 
-    pl.semaphore_wait(barrier, NE - 1 + 3 + NY - 1)
+    loads[3].wait()
+    loads[4].wait()
+    wi_t[...] = wi[...].T
+    wo_t[...] = wo[...].T
+    pl.semaphore_wait(barrier, NE + NZ)
 
     def out_half(q):
         def step(k, _):
@@ -157,18 +157,16 @@
         rows[0, q], rows[1, q] = apart(dst1[q])
         to_par[q].start()
     to_sib.start()
-    loads[3].wait()
-    loads[4].wait()
 
     def expert(i):
         at = pl.ds(2 * i, 2)
         value, slope = gelu_pair(dot(rows[0, at].reshape(NE, D), wi[...]))
         value = value.astype(BF16)
         act[i] = value
-        down = (dot(rows[1, at].reshape(NE, D), wo[...], WIDE) * slope).astype(BF16)
+        down = (dot(rows[1, at].reshape(NE, D), wo_t[...]) * slope).astype(BF16)
         pre_grad[i] = down
         part[0, at] = dot(value, wo[...]).astype(BF16).reshape(2, HALF, D)
-        part[1, at] = dot(down, wi[...], WIDE).astype(BF16).reshape(2, HALF, D)
+        part[1, at] = dot(down, wi_t[...]).astype(BF16).reshape(2, HALF, D)
 
     give = [
         copy(part.at[:, 5 + 2 * q], sib_in.at[:, 2 + q], p_s.at[q], p_r.at[q], sib) for q in range(2)
@@ -238,43 +236,42 @@
     gt[...] = grad.astype(BF16)
     store_t.start()
     k0.wait_recv()
-    mine = x * NZ + z
-    nxz = NX * NZ
-    key_split[...] = (key_mine[core] + key_sib[...]).astype(BF16).reshape(nxz, 2, D)
-
-    def plane_copy(src, dst, i, k):
-        xx, zz = plane(k)
-        return copy(src(xx * NZ + zz), dst, k_s.at[i], k_r.at[i], (g, xx * (NY * NZ) + y * NZ + zz))
+    key_split[...] = (key_mine[core] + key_sib[...]).astype(BF16).reshape(16, 4, D)
+    mine = ylo * NZ + z
 
     def scatter(k, _):
-        plane_copy(lambda t: key_split.at[t], key_got.at[mine], 1, k).start()
+        t, dev = near_by(k)
+        copy(key_split.at[t], key_got.at[mine], k_s.at[1], k_r.at[1], dev).start()
         return 0
 
-    lax.fori_loop(1, nxz, scatter, 0)
+    lax.fori_loop(1, 16, scatter, 0)
     key_got[pl.ds(mine, 1)] = key_split[pl.ds(mine, 1)]
-    k1 = copy(key_split.at[pl.ds(0, nxz - 1)], key_got.at[pl.ds(0, nxz - 1)], k_s.at[1], k_r.at[1], sib)
+    k1 = copy(key_split.at[pl.ds(0, 15)], key_got.at[pl.ds(0, 15)], k_s.at[1], k_r.at[1], sib)
     k1.wait_recv()
-    row = jnp.sum(key_got[...].astype(F32), axis=0)
-    place = 2 * y + ylo
-    key_row[...] = row
+    row = jnp.sum(key_got[...].astype(F32), axis=0).astype(BF16)
+    place = x * NY + y
+    key_row[...] = row[None]
     key_rows[pl.ds(place, 1)] = row[None]
 
-    for k in range(1, 8):
-        copy(key_row, key_rows.at[place], k_s.at[2], k_r.at[2], line(k)).start()
-    k2 = copy(key_rows.at[pl.ds(0, 7)], key_rows.at[pl.ds(0, 7)], k_s.at[2], k_r.at[2], sib)
+    def share(k, _):
+        copy(key_row.at[0], key_rows.at[place], k_s.at[2], k_r.at[2], far_off(k)).start()
+        return 0
+
+    lax.fori_loop(1, 16, share, 0)
+    k2 = copy(key_rows.at[pl.ds(0, 15)], key_rows.at[pl.ds(0, 15)], k_s.at[2], k_r.at[2], sib)
     k2.wait_recv()
-    row = jnp.sum(key_rows[...], axis=0).astype(BF16)
+    row = jnp.sum(key_rows[...].astype(F32), axis=0).astype(BF16)
     key_low[...] = row[None]
-    key_all[pl.ds(core * nxz + mine, 1)] = row[None]
+    key_all[pl.ds(core * 16 + mine, 1)] = row[None]
 
     def spread(k, _):
-        plane_copy(lambda t: key_low.at[0], key_all.at[core * nxz + mine], 3, k).start()
+        copy(key_low.at[0], key_all.at[core * 16 + mine], k_s.at[3], k_r.at[3], near_by(k)[1]).start()
         return 0
 
-    lax.fori_loop(1, nxz, spread, 0)
-    k3 = copy(key_split.at[pl.ds(0, nxz - 1)], key_got.at[pl.ds(0, nxz - 1)], k_s.at[3], k_r.at[3], sib)
+    lax.fori_loop(1, 16, spread, 0)
+    k3 = copy(key_split.at[pl.ds(0, 15)], key_got.at[pl.ds(0, 15)], k_s.at[3], k_r.at[3], sib)
     k3.wait_recv()
-    held = key_all.at[pl.ds(core * nxz, nxz)]
+    held = key_all.at[pl.ds(core * 16, 16)]
     k4 = copy(held, held, k_s.at[4], k_r.at[4], sib)
     k4.start()
     k4.wait_recv()
@@ -286,16 +283,27 @@
         done.wait_send()
 
 
-def hand_over(gt, gk, gwi, gwo, gt_out, gk_out, gwi_out, gwo_out, sem):
-    moves = [
-        pltpu.make_async_copy(a, b, sem.at[i])
-        for i, (a, b) in enumerate(((gwi, gwi_out), (gwo, gwo_out), (gt, gt_out)))
+def hand_over(gt, gk, gwi, gwo, gt_out, gk_out, gwi_out, gwo_out, t, k, turned, i, o, load_sem, store_sem):
+    def move(n, a, b):
+        return pltpu.make_async_copy(a, b, n)
+
+    loads = [
+        move(load_sem.at[n], a, b) for n, (a, b) in enumerate(((gk, k), (gt, t), (gwi, i), (gwo, o)))
     ]
-    for move in moves:
-        move.start()
-    gk_out[...] = gk[...].astype(F32).T
-    for move in moves:
-        move.wait()
+    stores = [
+        move(store_sem.at[n], a, b)
+        for n, (a, b) in enumerate(((turned, gk_out), (t, gt_out), (i, gwi_out), (o, gwo_out)))
+    ]
+    for load in loads:
+        load.start()
+    loads[0].wait()
+    turned[...] = k[...].astype(F32).T
+    stores[0].start()
+    for n in range(1, 4):
+        loads[n].wait()
+        stores[n].start()
+    for store in stores:
+        store.wait()
 
 
 def body(tokens, slot_keys, w_input, w_output, output_grad):
@@ -322,6 +330,8 @@
             pltpu.VMEM((256, D), BF16),
             pltpu.VMEM((D, D), BF16),
             pltpu.VMEM((D, D), BF16),
+            pltpu.VMEM((D, D), BF16),
+            pltpu.VMEM((D, D), BF16),
             pltpu.VMEM((256, n), F32),
             pltpu.VMEM((256, n), F32),
             pltpu.VMEM((n, n), BF16),
@@ -338,12 +348,12 @@
             pltpu.VMEM((n, 2, D), BF16),
             pltpu.VMEM((2, HALF, D), F32),
             pltpu.VMEM((HALF, D), F32),
-            pltpu.VMEM((NX * NZ, 2, D), BF16),
-            pltpu.VMEM((NX * NZ, 2, D), BF16),
-            pltpu.VMEM((2, D), F32),
-            pltpu.VMEM((8, 2, D), F32),
-            pltpu.VMEM((1, 2, D), BF16),
-            pltpu.VMEM((2 * NX * NZ, 2, D), BF16),
+            pltpu.VMEM((16, 4, D), BF16),
+            pltpu.VMEM((16, 4, D), BF16),
+            pltpu.VMEM((1, 4, D), BF16),
+            pltpu.VMEM((16, 4, D), BF16),
+            pltpu.VMEM((1, 4, D), BF16),
+            pltpu.VMEM((32, 4, D), BF16),
             dma((5,)), dma((3,)), dma((2,)), dma((2,)), dma((5,)), dma((5,)), dma((3,)), dma((3,)),
             dma((2,)), dma((2,)), dma, dma,
             dma((5,)), dma((5,)),
@@ -360,9 +370,18 @@
             jax.ShapeDtypeStruct((D, D), BF16),
             jax.ShapeDtypeStruct((D, D), BF16),
         ),
-        in_specs=[anywhere, vm, anywhere, anywhere],
-        out_specs=[anywhere, vm, anywhere, anywhere],
-        scratch_shapes=[dma((3,))],
+        in_specs=[anywhere] * 4,
+        out_specs=[anywhere] * 4,
+        scratch_shapes=[
+            pltpu.VMEM((256, D), BF16),
+            pltpu.VMEM((n, D), BF16),
+            pltpu.VMEM((D, n), F32),
+            pltpu.VMEM((D, D), BF16),
+            pltpu.VMEM((D, D), BF16),
+            dma((4,)),
+            dma((4,)),
+        ],
+        compiler_params=pltpu.CompilerParams(vmem_limit_bytes=60 << 20),
     )(gt, gk, gwi, gwo)
     return gt[None], gk, gwi[None], gwo[None]
 

time: 144 us -> 84.2 us (0.58)
  Pallas kernels: 143 us -> 83.4 us
    pallas_call x1, Pallas kernels: 62.3 us -> 2.57 us  [body(): pl.pallas_call(hand_over, out_shape=(jax.ShapeDtypeStruct((256, D), BF16)...]
where the time goes in v3:
time: 84.2 us; the launch traced here: 84 us
  Pallas kernels  83.4 us (99%)
    pallas_call x1, Pallas kernels, body(): pl.pallas_call(kernel, out_shape=(jax.ShapeDtypeStruct((256, D), BF16), j...  80.8 us
    pallas_call x1, Pallas kernels, body(): pl.pallas_call(hand_over, out_shape=(jax.ShapeDtypeStruct((256, D), BF16)...  2.57 us

profile of v3, /device:TPU:1, one launch (start us, length us, event | category | flops | bytes accessed | tf_op | source)
XLA Modules:
  0.0 84.0 jit_solution(4851479092845851404)
XLA Ops:
  0.6 80.8 %shard_map.84 = (bf16[256,640]{1,0:T(8,128)(2,1)}, bf16[128,640]{1,0:T(8,128)(2,1)}, bf16[640,640]{1,0:T(8,128)(2,1)}, bf16[640,640]{1,0:T(8,128)(2,1)}) custom-call(bf16[256,640]{1,0:T(8,128)(2,1)} %bitcast.9, bf16[640,128]{1,0:T(8,128)(2,1)} %keys_hbm.1, bf16[640,640]{1,0:T(8,128)(2,1)} %bitcast.7, bf16[640,640]{1,0:T(8,128)(2,1)} %bitcast.8, ...), custom_call_target="tpu_custom_call" | custom-call | tf_op jit(solution)/shard_map/pallas_call | solution.py:314
  81.5 2.6 %shard_map.85 = (bf16[256,640]{1,0:T(8,128)(2,1)}, f32[640,128]{1,0:T(8,128)}, bf16[640,640]{1,0:T(8,128)(2,1)}, bf16[640,640]{1,0:T(8,128)(2,1)}) custom-call(bf16[256,640]{1,0:T(8,128)(2,1)} %get-tuple-element.12.gt, bf16[128,640]{1,0:T(8,128)(2,1)} %get-tuple-element.13.gk, bf16[640,640]{1,0:T(8,128)(2,1)} %get-tuple-element.14.gwi, ...), custom_call_target="tpu_custom_call" | custom-call | tf_op jit(solution)/shard_map/pallas_call | solution.py:365

commit v4 on v3

--- a/solution.py
+++ b/solution.py
@@ -55,11 +55,20 @@
     sib = (g + 1 - 2 * core, e)
     par = ((g + 2) % 4, e)
 
-    def nth(q, k):
+    def index(xx, yy, zz):
+        return (xx % NX) * (NY * NZ) + (yy % NY) * NZ + zz % NZ
+
+    def turns(q, k):
         dy = ((k // 2) % 2) * 2 + (k // 16) % 2
         dx = ((k // 4) % 2) * 2 + (k // 32) % 2
-        dz = 2 * ((k % 2) * 2 + (k // 8) % 2) + (q + dx + dy) % 2
-        return ((x + dx) % NX) * (NY * NZ) + ((y + dy) % NY) * NZ + (z + dz) % NZ
+        return dx, dy, 2 * ((k % 2) * 2 + (k // 8) % 2) + (q + dx + dy) % 2
+
+    def lands(dx, dy, dz):
+        low = (dy // 2 + (1 - dy % 2) * ylo) % 2
+        return low * 2 + core, index(x + dx, y + dy, z + dz)
+
+    def slot_of(xx, yy, zz):
+        return (xx % NX) * (NY * NZ // 2) + (yy % NY) * (NZ // 2) + (zz % NZ) // 2
 
     def near_by(k):
         low, zz = (ylo + k // NZ) % 2, (z + k) % NZ
@@ -85,14 +94,24 @@
 
     barrier = pltpu.get_barrier_semaphore()
 
+    def hello(dev):
+        pl.semaphore_signal(barrier, inc=1, device_id=dev, device_id_type=MESH)
+
     def greet(k, _):
-        pl.semaphore_signal(barrier, inc=1, device_id=(g, (e + k) % NE), device_id_type=MESH)
+        hello(lands(k // (NY * NZ), (k // NZ) % NY, k % NZ))
         return 0
 
+    def greet_more(k, _):
+        hello((g, index(x + k // NZ, y + 3 - 2 * ylo, z + k % NZ)))
+        return 0
+
     lax.fori_loop(1, NE, greet, 0)
-    pl.semaphore_signal(barrier, inc=1, device_id=sib, device_id_type=MESH)
+    lax.fori_loop(0, NX * NZ, greet_more, 0)
+    for k in range(NX):
+        hello((g, index(x + k, y + 2, z)))
+    hello(sib)
     for k in range(NZ, 2 * NZ):
-        pl.semaphore_signal(barrier, inc=1, device_id=near_by(k)[1], device_id_type=MESH)
+        hello(near_by(k)[1])
 
     mix[...] = interleaver()
 
@@ -125,12 +144,14 @@
     loads[4].wait()
     wi_t[...] = wi[...].T
     wo_t[...] = wo[...].T
-    pl.semaphore_wait(barrier, NE + NZ)
+    pl.semaphore_wait(barrier, NE - 1 + NX * NZ + NX + 1 + NZ)
 
     def out_half(q):
         def step(k, _):
-            t = nth(q, k)
-            copy(src1.at[t], dst1.at[q, own], a1_s.at[q], a1_r.at[q], (g, t)).start()
+            dx, dy, dz = turns(q, k)
+            dev = lands(dx, dy, dz)
+            at = slot_of(x, y + (dy % 2) * (dy + 3 + 2 * ylo), z)
+            copy(src1.at[dev[1]], dst1.at[q, at], a1_s.at[q], a1_r.at[q], dev).start()
             return 0
 
         lax.fori_loop(1 - q, HALF, step, 0)
@@ -139,8 +160,13 @@
 
     def back_half(q):
         def step(k, _):
-            t = nth(q, k)
-            copy(src2.at[q, t // 2], dst2.at[e], a2_s, a2_r, (g, t)).start()
+            dx, dy, dz = turns(q, k)
+            odd, upper = dy % 2, dy // 2
+            low = (upper + odd + (1 - odd) * ylo) % 2
+            yy = y + odd * (3 + 2 * ylo) + (1 - odd) * dy
+            at = slot_of(x + dx, y + dy, z + dz)
+            dev = (low * 2 + core, index(x + dx, yy, z + dz))
+            copy(src2.at[q, at], dst2.at[e], a2_s, a2_r, dev).start()
             return 0
 
         lax.fori_loop(1 - q, HALF, step, 0)

time: 84.2 us -> 87.1 us (1.034)
  Pallas kernels: 83.4 us -> 86.3 us
    pallas_call x1, Pallas kernels: 80.8 us -> 83.7 us  [body(): pl.pallas_call(kernel, out_shape=(jax.ShapeDtypeStruct((256, D), BF16), j...]
where the time goes in v4:
time: 87.1 us; the launch traced here: 86.9 us
  Pallas kernels  86.3 us (99%)
    pallas_call x1, Pallas kernels, body(): pl.pallas_call(kernel, out_shape=(jax.ShapeDtypeStruct((256, D), BF16), j...  83.7 us
    pallas_call x1, Pallas kernels, body(): pl.pallas_call(hand_over, out_shape=(jax.ShapeDtypeStruct((256, D), BF16)...  2.57 us

profile of v4, /device:TPU:1, one launch (start us, length us, event | category | flops | bytes accessed | tf_op | source)
XLA Modules:
  0.0 86.9 jit_solution(6134732508845652755)
XLA Ops:
  0.6 83.7 %shard_map.84 = (bf16[256,640]{1,0:T(8,128)(2,1)}, bf16[128,640]{1,0:T(8,128)(2,1)}, bf16[640,640]{1,0:T(8,128)(2,1)}, bf16[640,640]{1,0:T(8,128)(2,1)}) custom-call(bf16[256,640]{1,0:T(8,128)(2,1)} %bitcast.9, bf16[640,128]{1,0:T(8,128)(2,1)} %keys_hbm.1, bf16[640,640]{1,0:T(8,128)(2,1)} %bitcast.7, bf16[640,640]{1,0:T(8,128)(2,1)} %bitcast.8, ...), custom_call_target="tpu_custom_call" | custom-call | tf_op jit(solution)/shard_map/pallas_call | solution.py:340
  84.4 2.6 %shard_map.85 = (bf16[256,640]{1,0:T(8,128)(2,1)}, f32[640,128]{1,0:T(8,128)}, bf16[640,640]{1,0:T(8,128)(2,1)}, bf16[640,640]{1,0:T(8,128)(2,1)}) custom-call(bf16[256,640]{1,0:T(8,128)(2,1)} %get-tuple-element.12.gt, bf16[128,640]{1,0:T(8,128)(2,1)} %get-tuple-element.13.gk, bf16[640,640]{1,0:T(8,128)(2,1)} %get-tuple-element.14.gwi, ...), custom_call_target="tpu_custom_call" | custom-call | tf_op jit(solution)/shard_map/pallas_call | solution.py:391

commit v5 on v3

--- a/solution.py
+++ b/solution.py
@@ -44,7 +44,7 @@
     tok_ref, keys_ref, wi, wo, og_ref, gt, gwi, gwo, wi_t, wo_t,
     dispatch, combine, mix,
     src1, dst1, rows, act, pre_grad, part, sib_in, chip_sum, par_in, src2, dst2,
-    key_mine, key_sib, key_split, key_got, key_row, key_rows, key_low, key_all,
+    key_mine, key_sent, key_sib, key_split, key_got, key_row, key_rows, key_low, key_all,
     w_sem, o_sem, a1_s, a1_r, g_s, g_r, p_s, p_r, c_s, c_r, a2_s, a2_r,
     k_s, k_r,
 ):
@@ -59,7 +59,9 @@
         dy = ((k // 2) % 2) * 2 + (k // 16) % 2
         dx = ((k // 4) % 2) * 2 + (k // 32) % 2
         dz = 2 * ((k % 2) * 2 + (k // 8) % 2) + (q + dx + dy) % 2
-        return ((x + dx) % NX) * (NY * NZ) + ((y + dy) % NY) * NZ + (z + dz) % NZ
+        way = 1 - 2 * core
+        xx, yy, zz = x + NX + way * dx, y + NY + way * dy, z + NZ + way * dz
+        return (xx % NX) * (NY * NZ) + (yy % NY) * NZ + zz % NZ
 
     def near_by(k):
         low, zz = (ylo + k // NZ) % 2, (z + k) % NZ
@@ -230,13 +232,14 @@
     term = dot(lg, tok, TALL)
 
     key_mine[...] = term.reshape(2, HALF, D)
-    k0 = copy(key_mine.at[1 - core], key_sib, k_s.at[0], k_r.at[0], sib)
+    key_sent[...] = key_mine[1 - core].astype(BF16)
+    k0 = copy(key_sent, key_sib, k_s.at[0], k_r.at[0], sib)
     k0.start()
     grad = dot(disp.astype(BF16), slot_in_grad) + dot(lg, keys_ref[...], WIDE)
     gt[...] = grad.astype(BF16)
     store_t.start()
     k0.wait_recv()
-    key_split[...] = (key_mine[core] + key_sib[...]).astype(BF16).reshape(16, 4, D)
+    key_split[...] = (key_mine[core] + key_sib[...].astype(F32)).astype(BF16).reshape(16, 4, D)
     mine = ylo * NZ + z
 
     def scatter(k, _):
@@ -347,7 +350,8 @@
             pltpu.VMEM((2, HALF, 2, D), BF16),
             pltpu.VMEM((n, 2, D), BF16),
             pltpu.VMEM((2, HALF, D), F32),
-            pltpu.VMEM((HALF, D), F32),
+            pltpu.VMEM((HALF, D), BF16),
+            pltpu.VMEM((HALF, D), BF16),
             pltpu.VMEM((16, 4, D), BF16),
             pltpu.VMEM((16, 4, D), BF16),
             pltpu.VMEM((1, 4, D), BF16),

time: 84.2 us -> 85.2 us (1.012)
  Pallas kernels: 83.4 us -> 84.4 us
    pallas_call x1, Pallas kernels: 80.8 us -> 81.8 us  [body(): pl.pallas_call(kernel, out_shape=(jax.ShapeDtypeStruct((256, D), BF16), j...]
where the time goes in v5:
time: 85.2 us; the launch traced here: 85 us
  Pallas kernels  84.4 us (99%)
    pallas_call x1, Pallas kernels, body(): pl.pallas_call(kernel, out_shape=(jax.ShapeDtypeStruct((256, D), BF16), j...  81.8 us
    pallas_call x1, Pallas kernels, body(): pl.pallas_call(hand_over, out_shape=(jax.ShapeDtypeStruct((256, D), BF16)...  2.57 us

profile of v5, /device:TPU:1, one launch (start us, length us, event | category | flops | bytes accessed | tf_op | source)
XLA Modules:
  0.0 85.0 jit_solution(567838148054792884)
XLA Ops:
  0.6 81.8 %shard_map.84 = (bf16[256,640]{1,0:T(8,128)(2,1)}, bf16[128,640]{1,0:T(8,128)(2,1)}, bf16[640,640]{1,0:T(8,128)(2,1)}, bf16[640,640]{1,0:T(8,128)(2,1)}) custom-call(bf16[256,640]{1,0:T(8,128)(2,1)} %bitcast.9, bf16[640,128]{1,0:T(8,128)(2,1)} %keys_hbm.1, bf16[640,640]{1,0:T(8,128)(2,1)} %bitcast.7, bf16[640,640]{1,0:T(8,128)(2,1)} %bitcast.8, ...), custom_call_target="tpu_custom_call" | custom-call | tf_op jit(solution)/shard_map/pallas_call | solution.py:317
  82.5 2.6 %shard_map.85 = (bf16[256,640]{1,0:T(8,128)(2,1)}, f32[640,128]{1,0:T(8,128)}, bf16[640,640]{1,0:T(8,128)(2,1)}, bf16[640,640]{1,0:T(8,128)(2,1)}) custom-call(bf16[256,640]{1,0:T(8,128)(2,1)} %get-tuple-element.12.gt, bf16[128,640]{1,0:T(8,128)(2,1)} %get-tuple-element.13.gk, bf16[640,640]{1,0:T(8,128)(2,1)} %get-tuple-element.14.gwi, ...), custom_call_target="tpu_custom_call" | custom-call | tf_op jit(solution)/shard_map/pallas_call | solution.py:369

commit v6 on v3

--- a/solution.py
+++ b/solution.py
@@ -56,6 +56,7 @@
     par = ((g + 2) % 4, e)
 
     def nth(q, k):
+        k = HALF - q - k
         dy = ((k // 2) % 2) * 2 + (k // 16) % 2
         dx = ((k // 4) % 2) * 2 + (k // 32) % 2
         dz = 2 * ((k % 2) * 2 + (k // 8) % 2) + (q + dx + dy) % 2

time: 84.2 us -> 85.8 us (1.019)
  Pallas kernels: 83.4 us -> 85 us
    pallas_call x1, Pallas kernels: 80.8 us -> 82.4 us  [body(): pl.pallas_call(kernel, out_shape=(jax.ShapeDtypeStruct((256, D), BF16), j...]
where the time goes in v6:
time: 85.8 us; the launch traced here: 85.6 us
  Pallas kernels  85 us (99%)
    pallas_call x1, Pallas kernels, body(): pl.pallas_call(kernel, out_shape=(jax.ShapeDtypeStruct((256, D), BF16), j...  82.4 us
    pallas_call x1, Pallas kernels, body(): pl.pallas_call(hand_over, out_shape=(jax.ShapeDtypeStruct((256, D), BF16)...  2.57 us

profile of v6, /device:TPU:1, one launch (start us, length us, event | category | flops | bytes accessed | tf_op | source)
XLA Modules:
  0.0 85.6 jit_solution(221612241409785560)
XLA Ops:
  0.6 82.4 %shard_map.84 = (bf16[256,640]{1,0:T(8,128)(2,1)}, bf16[128,640]{1,0:T(8,128)(2,1)}, bf16[640,640]{1,0:T(8,128)(2,1)}, bf16[640,640]{1,0:T(8,128)(2,1)}) custom-call(bf16[256,640]{1,0:T(8,128)(2,1)} %bitcast.9, bf16[640,128]{1,0:T(8,128)(2,1)} %keys_hbm.1, bf16[640,640]{1,0:T(8,128)(2,1)} %bitcast.7, bf16[640,640]{1,0:T(8,128)(2,1)} %bitcast.8, ...), custom_call_target="tpu_custom_call" | custom-call | tf_op jit(solution)/shard_map/pallas_call | solution.py:315
  83.1 2.6 %shard_map.85 = (bf16[256,640]{1,0:T(8,128)(2,1)}, f32[640,128]{1,0:T(8,128)}, bf16[640,640]{1,0:T(8,128)(2,1)}, bf16[640,640]{1,0:T(8,128)(2,1)}) custom-call(bf16[256,640]{1,0:T(8,128)(2,1)} %get-tuple-element.12.gt, bf16[128,640]{1,0:T(8,128)(2,1)} %get-tuple-element.13.gk, bf16[640,640]{1,0:T(8,128)(2,1)} %get-tuple-element.14.gwi, ...), custom_call_target="tpu_custom_call" | custom-call | tf_op jit(solution)/shard_map/pallas_call | solution.py:366
